TPU v7x, 32 devices: a whole 2x2x4 slice. The times are simulated.
32 devices in a mesh: expert: 16 (over z, y, core), dp: 2 (over x).
Axes of the slice: x: 2, y: 2, z: 4, core: 2. Of those that a mesh axis runs over, the one named last changes fastest.
Arguments:
- tokens: bfloat16 [16, 7168], P('dp', 'expert'), may hold values from -6 to 6
- expert_ids: int32 [16, 8], P('dp'), may hold values from 0 to 15, all different within a row; in each aligned block of 8 rows (0 to 7, 8 to 15, ...) at most 8 rows name the same one
- gate_values: float32 [16, 8], P('dp'), may hold values from 0.05 to 1
- w_gate: bfloat16 [16, 2048, 7168], P('expert', 'dp'), may hold values from -0.0625 to 0.0625
- w_up: bfloat16 [16, 2048, 7168], P('expert', 'dp'), may hold values from -0.0625 to 0.0625
- w_down: bfloat16 [16, 2048, 7168], P('expert', 'dp'), may hold values from -0.125 to 0.125
Outputs:
- mixed: bfloat16 [16, 7168], P('dp', 'expert')
Inputs may be any that keep to these rules, and one draw needn't show every extreme that they name: `expert_ids`: each token names 8 different experts; among the 8 tokens of one index of dp no expert is named more than 8 times, and in every draw some expert is named exactly 8 times by one such block.
All inputs are finite; a program needn't handle non-finite values.
Results may differ from a plain program's by a relative error of at most 0.0051.
Values may be sent and summed in bfloat16 or wider, within the bound.
A program may use at most 192 MiB of HBM per device.

v0:
```python
import jax
import jax.numpy as jnp
from jax import lax
from jax.sharding import PartitionSpec as P


def against_features(piece, weight):
    return lax.dot_general(
        piece, weight, (((1,), (1,)), ((), ())), preferred_element_type=jnp.float32
    )


def local(tokens, expert_ids, gate_values, w_gate, w_up, w_down):
    n_expert = lax.axis_size("expert")
    tok_count, feat_cols = tokens.shape
    choose = expert_ids.shape[1]
    capacity = min(tok_count, max(2, 2 * tok_count * choose // n_expert))
    flat = expert_ids.reshape(-1)
    onehot = (flat[:, None] == jnp.arange(n_expert, dtype=jnp.int32)[None, :]).astype(jnp.int32)
    rank = jnp.cumsum(onehot, axis=0) - onehot
    target = flat * capacity + jnp.sum(rank * onehot, axis=1)
    place = target[:, None] == jnp.arange(n_expert * capacity, dtype=jnp.int32)[None, :]
    owner = (jnp.arange(tok_count * choose) // choose)[:, None] == jnp.arange(tok_count)[None, :]
    routing = jnp.dot(
        place.T.astype(jnp.bfloat16), owner.astype(jnp.bfloat16), preferred_element_type=jnp.float32
    )
    slots = jnp.dot(
        routing.astype(jnp.bfloat16), tokens, preferred_element_type=jnp.float32
    ).astype(jnp.bfloat16)
    slots = slots.reshape(n_expert, capacity, feat_cols)
    arrived = lax.all_to_all(slots, "expert", split_axis=0, concat_axis=2, tiled=True)
    rows = arrived.reshape(capacity, -1)
    gate_local = w_gate[0]
    up_local = w_up[0]
    down_local = w_down[0]
    piece = lax.all_gather(rows, "dp", axis=0, tiled=True)
    gate = against_features(piece, gate_local)
    upper = against_features(piece, up_local)
    hidden_all = (jax.nn.silu(gate) * upper).astype(jnp.bfloat16)
    parts = jnp.dot(hidden_all, down_local, preferred_element_type=jnp.float32)
    back = lax.psum_scatter(parts, "dp", scatter_dimension=0, tiled=True)
    home = lax.all_to_all(
        back.reshape(1, capacity, -1), "expert", split_axis=2, concat_axis=0, tiled=True
    )
    home = home.reshape(n_expert * capacity, feat_cols)
    picked = jnp.take(home, target, axis=0)
    weighted = picked * gate_values.reshape(-1)[:, None]
    mixed = jnp.sum(weighted.reshape(tok_count, choose, feat_cols), axis=1)
    return mixed.astype(jnp.bfloat16)


def solution(mesh):
    placed = (
        P("dp", "expert"),
        P("dp", None),
        P("dp", None),
        P("expert", "dp", None),
        P("expert", "dp", None),
        P("expert", "dp", None),
    )
    return jax.shard_map(
        local, mesh=mesh, in_specs=placed, out_specs=P("dp", "expert"), check_vma=False
    )
```

profile of v0, /device:TPU:0, one launch (start us, length us, event | category | flops | bytes accessed | tf_op | source)
XLA Modules:
  0.0 145.1 jit_solution(16538417424236382855)
XLA Ops:
  6.5 0.0 copy-start
  6.5 0.0 reduce-scatter.2.cloned.1.call-start
  6.5 0.8 reshape.84
  7.3 0.1 fusion.22
  7.4 0.1 reduce_window_sum.11
  7.5 0.2 select_reduce_fusion
  7.7 0.0 copy-done
  7.7 0.4 convolution_convert_fusion
  8.1 0.1 copy.11
  8.2 15.1 %all_to_all.30 = bf16[16,8,448]{2,1,0:T(8,128)(2,1)S(1)} all-to-all(bf16[16,8,448]{2,1,0:T(8,128)(2,1)S(1)} %bitcast.46), channel_id=1, replica_groups=mesh['expert'=16,'dp'=2] {'expert'}, dimensions={0} | all-to-all | bytes 229376 | tf_op jit(solution)/shard_map/all_to_all | solution.py:31
  23.4 0.2 reshape.86
  23.6 5.5 %all_gather.3 = bf16[16,7168]{1,0:T(8,128)(2,1)S(1)} all-gather(bf16[8,7168]{1,0:T(8,128)(2,1)S(1)} %reshape.86), channel_id=1, replica_groups=mesh['expert'=16,'dp'=2] {'dp'}, dimensions={0}, use_global_device_ids=true | all-gather | bytes 344064 | tf_op jit(solution)/shard_map/all_gather | solution.py:36
  29.0 9.1 %fusion.4 = f32[16,1024]{1,0:T(8,128)S(1)} fusion(bf16[16,7168]{1,0:T(8,128)(2,1)S(1)} %all_gather.3, bf16[1,1024,7168]{2,1,0:T(8,128)(2,1)} %param.9), kind=kOutput, calls=%fused_computation.5 | convolution fusion | flops 234881024 | bytes 14974976 | tf_op jit(solution)/shard_map/dot_general | solution.py:8
  38.1 0.0 copy-start.1
  38.1 13.4 %fusion = f32[16,7168]{1,0:T(8,128)} fusion(bf16[1,1024,7168]{2,1,0:T(8,128)(2,1)} %param.11, bf16[16,7168]{1,0:T(8,128)(2,1)S(1)} %all_gather.3, bf16[1,1024,7168]{2,1,0:T(8,128)(2,1)} %param.10, f32[16,1024]{1,0:T(8,128)S(1)} %fusion.4), kind=kOutput, calls=%fused_computation.1 | convolution fusion | flops 469860352 | bytes 30113792 | tf_op jit(solution)/shard_map/dot_general | solution.py:40
  51.4 0.0 copy-start.2
  51.4 0.0 reduce-scatter.2.cloned.1.call-update
  51.5 0.0 copy-done.1
  51.5 0.1 mul.52
  51.6 11.9 %reduce-scatter.2.cloned.1.call-done = f32[8,7168]{1,0:T(8,128)} async-done(((f32[16,7168]{1,0:T(8,128)}), f32[8,7168]{1,0:T(8,128)}) %reduce-scatter.2.cloned.1.call-update) | async-done | bytes 229392 | tf_op jit(solution)/shard_map/reduce_scatter | solution.py:41
  63.5 7.3 %copy.13 = f32[1,8,7168]{1,0,2:T(1,128)} copy(f32[1,8,7168]{2,1,0:T(8,128)} %bitcast.48) | data formatting | bytes 458752 | tf_op jit(solution)/shard_map/reshape | solution.py:43
  70.8 0.5 broadcast.89
  71.3 33.9 %reduce = f32[7168,8]{1,0:T(8,128)} reduce(f32[7168,1,8]{2,1,0:T(1,128)} %bitcast.43, f32[]{:T(128)} %broadcast.89), dimensions={1}, to_apply=%bitcast.38.reduce_sub_computation | reduce | bytes 458756
  105.2 4.2 %reshape.97 = f32[16,1,3584]{2,1,0:T(1,128)} reshape(f32[7168,8]{1,0:T(8,128)} %reduce) | data formatting | bytes 458752
  109.4 5.6 %all-to-all-start.1 = ((f32[16,1,3584]{2,1,0:T(1,128)}), f32[16,1,3584]{2,1,0:T(1,128)S(1)}, u32[]{:S(2)}, u32[]{:S(2)}) async-start(f32[16,1,3584]{2,1,0:T(1,128)} %reshape.97), calls=%async_computation.2 | async-start | bytes 458752 | tf_op jit(solution)/shard_map/all_to_all | solution.py:42
  115.1 0.1 reduce_sum.23
  115.2 9.4 %all-to-all-done.1 = f32[16,1,3584]{2,1,0:T(1,128)S(1)} async-done(((f32[16,1,3584]{2,1,0:T(1,128)}), f32[16,1,3584]{2,1,0:T(1,128)S(1)}, u32[]{:S(2)}, u32[]{:S(2)}) %all-to-all-start.1) | async-done | bytes 229408 | tf_op jit(solution)/shard_map/all_to_all | solution.py:42
  124.6 1.2 reduce.1
  125.8 8.4 %reshape.98 = f32[7168,1,8]{2,1,0:T(1,128)} reshape(f32[16,3584]{1,0:T(8,128)S(1)} %reduce.1) | data formatting | bytes 458752
  134.2 2.6 %copy.14 = f32[1,8,16,448]{3,1,2,0:T(8,128)S(1)} copy(f32[1,8,16,448]{1,3,2,0:T(8,128)} %bitcast.44) | data formatting | bytes 458752 | tf_op jit(solution)/shard_map/all_to_all | solution.py:42
  136.8 0.7 gather_fusion
  137.5 0.0 copy-done.2
  137.5 0.7 fusion.15
  (6 shorter events, 0.1 us)
Async XLA Ops:
  6.5 1.2 copy-start
  6.5 57.0 %reduce-scatter.2.cloned.1.call-start = ((), (), s32[]{:S(2)}) async-start(), calls=%async_computation.3 | async-start | bytes 688128 | tf_op jit(solution)/shard_map/reduce_scatter | solution.py:41
  38.1 13.4 %copy-start.1 = (s32[8,8]{1,0:T(8,128)S(1)}, s32[8,8]{1,0:T(8,128)}, u32[]{:S(2)}) copy-start(s32[8,8]{1,0:T(8,128)} %param.7) | copy-start | bytes 772
  51.4 86.1 %copy-start.2 = (f32[8,8]{1,0:T(8,128)S(1)}, f32[8,8]{1,0:T(8,128)}, u32[]{:S(2)}) copy-start(f32[8,8]{1,0:T(8,128)} %param.8) | copy-start | bytes 772
  109.4 15.1 %all-to-all-start.1 = ((f32[16,1,3584]{2,1,0:T(1,128)}), f32[16,1,3584]{2,1,0:T(1,128)S(1)}, u32[]{:S(2)}, u32[]{:S(2)}) async-start(f32[16,1,3584]{2,1,0:T(1,128)} %reshape.97), calls=%async_computation.2 | async-start | bytes 458752 | tf_op jit(solution)/shard_map/all_to_all | solution.py:42
Sparse Core Ops, SparseCore 0:
  51.6 11.8 reduce-scatter.1
where the time goes:
time: 146 us; the launch traced here: 145 us
  other arithmetic  36.2 us (25%)
  local copies, waits for them, and re-layouts  25 us (17%)
  matrix products  22.8 us (16%)
  waiting for transfers between devices  21.3 us (15%)
  blocking collectives  20.6 us (14%)
  between operations  13.5 us (9%)
  starting transfers between devices  5.62 us (4%)
    unnamed x1, other arithmetic  33.9 us
    all_to_all x1, blocking collectives, local(): lax.all_to_all(slots, 'expert', split_axis=0, concat_axis=2, tiled=True)  15.1 us
    dot_general x1, matrix products, local(): parts = jnp.dot(hidden_all, down_local, preferred_element_type=jnp.float32)  13.4 us
    unnamed x9, local copies, waits for them, and re-layouts  13.2 us
    reduce_scatter x1, waiting for transfers between devices, local(): back = lax.psum_scatter(parts, 'dp', scatter_dimension=0, tiled=True)  11.9 us
    all_to_all x1, waiting for transfers between devices, local(): lax.all_to_all(back.reshape(1, capacity, -1), 'expert', split_axis=2, con...  9.4 us
    dot_general x1, matrix products, against_features(): lax.dot_general(piece, weight, (((1,), (1,)), ((), ())), preferred_elemen...  9.05 us
    reshape x1, local copies, waits for them, and re-layouts, local(): back.reshape(1, capacity, -1)  7.3 us
  transfers between devices with their start and end apart: 2, of which 2 were waited for; matrix products, arithmetic and copies ran while one was open for 0% of the time, Pallas kernels for 0%

commit v1 on v0

v1 whole, which is shorter than its diff:
```python
import functools

import jax
import jax.numpy as jnp
from jax import lax
from jax.experimental import pallas as pl
from jax.experimental.pallas import tpu as pltpu
from jax.sharding import PartitionSpec as P

MESH = pl.DeviceIdType.MESH


def against_features(piece, weight):
    return lax.dot_general(
        piece, weight, (((1,), (1,)), ((), ())), preferred_element_type=jnp.float32
    )


def each(count, body):
    if count <= 4:
        for i in range(count):
            body(i)
    else:
        @pl.loop(0, count)
        def _(i):
            body(i)


def fold(block):
    half = block.shape[1] // 2
    return jnp.concatenate([block[:, :half], block[:, half:]], axis=0)


def unfold(block):
    half = block.shape[0] // 2
    return jnp.concatenate([block[:half], block[half:]], axis=1)


def kernel(
    n_exp, n_dp, hid_block, col_block,
    tok_ref, ids_ref, gates_ref, wg_hbm, wu_hbm, wd_hbm, out_ref,
    wg, wu, wd, stage, tokbuf, x, hid, y, sendbuf, recvbuf,
    g_sem, u_sem, d_sem, tok_send, tok_recv, out_send, out_recv,
):
    n_all = n_exp * n_dp
    rows, cols = tok_ref.shape
    n_hid = wg.shape[0]
    n_col = wd.shape[0]
    per = col_block // cols
    e_me = lax.axis_index("expert")
    d_me = lax.axis_index("dp")
    me = e_me * n_dp + d_me
    home = e_me // per

    def chunk_at(i):
        i = jnp.int32(i)
        turn = n_col // 2 + (1 - 2 * (i % 2)) * ((i + 1) // 2)
        return (home + turn) % n_col

    def copy_gate(i):
        at = pl.ds(i * hid_block, hid_block)
        return pltpu.make_async_copy(wg_hbm.at[at], wg.at[i], g_sem.at[i])

    def copy_up(i):
        at = pl.ds(i * hid_block, hid_block)
        return pltpu.make_async_copy(wu_hbm.at[at], wu.at[i], u_sem.at[i])

    def copy_down(i):
        start = pl.multiple_of(chunk_at(i) * col_block, 128)
        return pltpu.make_async_copy(
            wd_hbm.at[:, pl.ds(start, col_block)], wd.at[i], d_sem.at[i]
        )

    barrier = pltpu.get_barrier_semaphore()

    @pl.loop(1, n_all)
    def _(k):
        to = (me + k) % n_all
        pl.semaphore_signal(
            barrier, inc=1, device_id=(to // n_dp, to % n_dp), device_id_type=MESH
        )

    for i in range(n_hid):
        copy_gate(i).start()
        copy_up(i).start()
    for i in range(n_col):
        copy_down(i).start()

    stage[...] = fold(tok_ref[...].astype(jnp.float32)).astype(jnp.bfloat16)
    own = pltpu.make_async_copy(stage, tokbuf.at[me], tok_recv)
    own.start()
    pl.semaphore_wait(barrier, n_all - 1)

    @pl.loop(1, n_all)
    def _(k):
        to = (me + k) % n_all
        pltpu.make_async_remote_copy(
            src_ref=stage, dst_ref=tokbuf.at[me], send_sem=tok_send, recv_sem=tok_recv,
            device_id=(to // n_dp, to % n_dp), device_id_type=MESH,
        ).start()

    pltpu.make_async_copy(tokbuf, tokbuf, tok_recv).wait()

    def gather_rows(pair):
        halves = []
        for q in range(2):
            parts = [
                unfold(tokbuf[e * n_dp + pair * 2 + q].astype(jnp.float32))
                for e in range(n_exp)
            ]
            halves.append(jnp.concatenate(parts, axis=1))
        both = jnp.concatenate(halves, axis=0).astype(jnp.bfloat16)
        x[pl.ds(pair * 2 * rows, 2 * rows), :] = both

    each(n_dp // 2, gather_rows)

    @pl.loop(0, n_hid)
    def _(i):
        copy_gate(i).wait()
        gate = against_features(x[...], wg[i])
        copy_up(i).wait()
        upper = against_features(x[...], wu[i])
        hid[i] = (gate / (1.0 + jnp.exp(-gate)) * upper).astype(jnp.bfloat16)

    @pl.loop(0, n_col)
    def _(i):
        chunk = chunk_at(i)
        copy_down(i).wait()
        h = jnp.concatenate([hid[j] for j in range(n_hid)], axis=1)
        y[...] = jnp.dot(h, wd[i], preferred_element_type=jnp.float32)

        def send(d):
            for p in range(per):
                e_to = chunk * per + p
                to = e_to * n_dp + d
                block = y[pl.ds(d * rows, rows), p * cols:(p + 1) * cols]
                sendbuf[to] = fold(block).astype(jnp.bfloat16)

                @pl.when(to != me)
                def _():
                    pltpu.make_async_remote_copy(
                        src_ref=sendbuf.at[to], dst_ref=recvbuf.at[me],
                        send_sem=out_send, recv_sem=out_recv,
                        device_id=(e_to, d), device_id_type=MESH,
                    ).start()

                @pl.when(to == me)
                def _():
                    pltpu.make_async_copy(sendbuf.at[to], recvbuf.at[me], out_recv).start()

        each(n_dp, send)

    ids = ids_ref[...]
    gates = gates_ref[...]
    shares = []
    for e in range(n_exp):
        one = jnp.sum(jnp.where(ids == e, gates, 0.0), axis=1, keepdims=True)
        shares.append(jnp.concatenate([one, one], axis=0))
    pltpu.make_async_copy(recvbuf, recvbuf, out_recv).wait()
    total = jnp.zeros((2 * rows, cols // 2), jnp.float32)
    for e in range(n_exp):
        part = jnp.zeros((2 * rows, cols // 2), jnp.float32)
        for d in range(n_dp):
            part = part + recvbuf[e * n_dp + d].astype(jnp.float32)
        total = total + part * shares[e]
    out_ref[...] = unfold(total).astype(out_ref.dtype)

    pltpu.make_async_copy(
        tokbuf.at[pl.ds(0, n_all - 1)], tokbuf.at[pl.ds(0, n_all - 1)], tok_send
    ).wait()
    pltpu.make_async_copy(
        sendbuf.at[pl.ds(0, n_all - 1)], sendbuf.at[pl.ds(0, n_all - 1)], out_send
    ).wait()


def local(n_exp, n_dp, tokens, expert_ids, gate_values, w_gate, w_up, w_down):
    rows, cols = tokens.shape
    _, hidden, width = w_gate.shape
    all_rows = rows * n_dp
    n_all = n_exp * n_dp
    hid_block = min(256, hidden)
    col_block = cols
    while col_block % 128:
        col_block *= 2
    n_hid, n_col = hidden // hid_block, width // col_block
    vmem = pl.BlockSpec(memory_space=pltpu.VMEM)
    hbm = pl.BlockSpec(memory_space=pl.ANY)
    bf16, f32 = jnp.bfloat16, jnp.float32
    return pl.pallas_call(
        functools.partial(kernel, n_exp, n_dp, hid_block, col_block),
        out_shape=jax.ShapeDtypeStruct((rows, cols), bf16),
        in_specs=[vmem, vmem, vmem, hbm, hbm, hbm],
        out_specs=vmem,
        scratch_shapes=[
            pltpu.VMEM((n_hid, hid_block, width), bf16),
            pltpu.VMEM((n_hid, hid_block, width), bf16),
            pltpu.VMEM((n_col, hidden, col_block), bf16),
            pltpu.VMEM((2 * rows, cols // 2), bf16),
            pltpu.VMEM((n_all, 2 * rows, cols // 2), bf16),
            pltpu.VMEM((all_rows, width), bf16),
            pltpu.VMEM((n_hid, all_rows, hid_block), bf16),
            pltpu.VMEM((all_rows, col_block), f32),
            pltpu.VMEM((n_all, 2 * rows, cols // 2), bf16),
            pltpu.VMEM((n_all, 2 * rows, cols // 2), bf16),
            pltpu.SemaphoreType.DMA((n_hid,)),
            pltpu.SemaphoreType.DMA((n_hid,)),
            pltpu.SemaphoreType.DMA((n_col,)),
            pltpu.SemaphoreType.DMA,
            pltpu.SemaphoreType.DMA,
            pltpu.SemaphoreType.DMA,
            pltpu.SemaphoreType.DMA,
        ],
        compiler_params=pltpu.CompilerParams(
            collective_id=0, has_side_effects=True, vmem_limit_bytes=56 * 1024 * 1024
        ),
    )(tokens, expert_ids, gate_values, w_gate[0], w_up[0], w_down[0])


def solution(mesh):
    placed = (
        P("dp", "expert"),
        P("dp", None),
        P("dp", None),
        P("expert", "dp", None),
        P("expert", "dp", None),
        P("expert", "dp", None),
    )
    return jax.shard_map(
        functools.partial(local, mesh.shape["expert"], mesh.shape["dp"]),
        mesh=mesh, in_specs=placed, out_specs=P("dp", "expert"), check_vma=False,
    )
```

time: 146 us -> 43.2 us (0.30)
  Pallas kernels: 0 us -> 41.6 us
  other arithmetic: 36.2 us -> 0 us
  local copies, waits for them, and re-layouts: 25 us -> 1.3 us
  matrix products: 22.8 us -> 0 us
  waiting for transfers between devices: 21.3 us -> 0 us
  blocking collectives: 20.6 us -> 0 us
  between operations: 13.5 us -> 0.01 us
  starting transfers between devices: 5.62 us -> 0 us
    pallas_call x0 -> x1, Pallas kernels: none -> 41.6 us  [local(): pl.pallas_call(functools.partial(kernel, n_exp, n_dp, hid_block, col_bloc...]
    unnamed x1 -> x0, other arithmetic: 33.9 us -> none
    dot_general x3 -> x0, matrix products: 22.8 us -> none  [the longest x1 13.4 us: local(): parts = jnp.dot(hidden_all, down_local, preferred_element_type=jnp.float32)]
    all_to_all x1 -> x0, blocking collectives: 15.1 us -> none  [local(): lax.all_to_all(slots, 'expert', split_axis=0, concat_axis=2, tiled=True)]
    reduce_scatter x1 -> x0, waiting for transfers between devices: 11.9 us -> none  [local(): back = lax.psum_scatter(parts, 'dp', scatter_dimension=0, tiled=True)]
    unnamed x9 -> x1, local copies, waits for them, and re-layouts: 13.2 us -> 1.3 us
    all_to_all x1 -> x0, waiting for transfers between devices: 9.4 us -> none  [local(): lax.all_to_all(back.reshape(1, capacity, -1), 'expert', split_axis=2, con...]
    reshape x3 -> x0, local copies, waits for them, and re-layouts: 8.23 us -> none  [the longest x1 7.3 us: local(): back.reshape(1, capacity, -1)]
  transfers between devices with their start and end apart: 2 -> 0, of which waited for: 2 -> 0; matrix products, arithmetic and copies ran while one was open for 0% -> 0% of each run, Pallas kernels for 0% -> 0%
where the time goes in v1:
time: 43.2 us; the launch traced here: 42.9 us
  Pallas kernels  41.6 us (96%)
  local copies, waits for them, and re-layouts  1.3 us (3%)
    pallas_call x1, Pallas kernels, local(): pl.pallas_call(functools.partial(kernel, n_exp, n_dp, hid_block, col_bloc...  41.6 us
    unnamed x1, local copies, waits for them, and re-layouts  1.3 us

profile of v1, /device:TPU:0, one launch (start us, length us, event | category | flops | bytes accessed | tf_op | source)
XLA Modules:
  0.0 42.9 jit_solution(12540324705890256901)
XLA Ops:
  0.0 41.6 %shard_map.64 = bf16[8,448]{1,0:T(8,128)(2,1)} custom-call(bf16[8,448]{1,0:T(8,128)(2,1)} %tok_ref.1, s32[8,8]{1,0:T(8,128)} %ids_ref.1, f32[8,8]{1,0:T(8,128)} %gates_ref.1, bf16[1024,7168]{1,0:T(8,128)(2,1)} %bitcast.3, bf16[1024,7168]{1,0:T(8,128)(2,1)} %bitcast.4, bf16[1024,7168]{1,0:T(8,128)(2,1)} %bitcast.5), custom_call_target="tpu_custom_call" | custom-call | tf_op jit(solution)/shard_map/pallas_call | solution.py:189
  41.6 1.3 %copy.8 = bf16[8,448]{1,0:T(8,128)(2,1)} copy(bf16[8,448]{1,0:T(8,128)(2,1)} %shard_map.64) | data formatting | bytes 14336

commit v2 on v1

--- a/solution.py
+++ b/solution.py
@@ -8,12 +8,21 @@
 from jax.sharding import PartitionSpec as P
 
 MESH = pl.DeviceIdType.MESH
+AHEAD = 2
+EARLY = 2
 
 
 def against_features(piece, weight):
     return lax.dot_general(
         piece, weight, (((1,), (1,)), ((), ())), preferred_element_type=jnp.float32
     )
+
+
+def spans(cols, col_block):
+    first = [p * cols // 128 * 128 for p in range(col_block // cols)]
+    need = max(p * cols - start + cols for p, start in enumerate(first))
+    width = -(-need // 256) * 256
+    return [min(start, col_block - width) for start in first], width
 
 
 def each(count, body):
@@ -47,6 +56,9 @@
     n_hid = wg.shape[0]
     n_col = wd.shape[0]
     per = col_block // cols
+    n_pair = n_col // 2
+    starts, span = spans(cols, col_block)
+    early = min(EARLY, n_hid)
     e_me = lax.axis_index("expert")
     d_me = lax.axis_index("dp")
     me = e_me * n_dp + d_me
@@ -80,11 +92,27 @@
             barrier, inc=1, device_id=(to // n_dp, to % n_dp), device_id_type=MESH
         )
 
-    for i in range(n_hid):
+    def start_hid(i):
         copy_gate(i).start()
         copy_up(i).start()
-    for i in range(n_col):
-        copy_down(i).start()
+
+    def start_step(i):
+        if isinstance(i, int):
+            if i < n_hid:
+                start_hid(i)
+            elif i < n_hid + n_pair:
+                copy_down(2 * (i - n_hid)).start()
+                copy_down(2 * (i - n_hid) + 1).start()
+            return
+        pl.when(i < n_hid)(lambda: start_hid(i))
+
+        @pl.when((i >= n_hid) & (i < n_hid + n_pair))
+        def _():
+            copy_down(2 * (i - n_hid)).start()
+            copy_down(2 * (i - n_hid) + 1).start()
+
+    for i in range(AHEAD):
+        start_step(i)
 
     stage[...] = fold(tok_ref[...].astype(jnp.float32)).astype(jnp.bfloat16)
     own = pltpu.make_async_copy(stage, tokbuf.at[me], tok_recv)
@@ -99,6 +127,10 @@
             device_id=(to // n_dp, to % n_dp), device_id_type=MESH,
         ).start()
 
+    for i in range(early):
+        copy_gate(i).wait()
+        copy_up(i).wait()
+        start_step(i + AHEAD)
     pltpu.make_async_copy(tokbuf, tokbuf, tok_recv).wait()
 
     def gather_rows(pair):
@@ -116,9 +148,13 @@
 
     @pl.loop(0, n_hid)
     def _(i):
-        copy_gate(i).wait()
+        @pl.when(i >= early)
+        def _():
+            copy_gate(i).wait()
+            copy_up(i).wait()
+            start_step(i + AHEAD)
+
         gate = against_features(x[...], wg[i])
-        copy_up(i).wait()
         upper = against_features(x[...], wu[i])
         hid[i] = (gate / (1.0 + jnp.exp(-gate)) * upper).astype(jnp.bfloat16)
 
@@ -126,6 +162,7 @@
     def _(i):
         chunk = chunk_at(i)
         copy_down(i).wait()
+        pl.when(i % 2 == 1)(lambda: start_step(n_hid + i // 2 + AHEAD))
         h = jnp.concatenate([hid[j] for j in range(n_hid)], axis=1)
         y[...] = jnp.dot(h, wd[i], preferred_element_type=jnp.float32)
 
@@ -133,7 +170,7 @@
             for p in range(per):
                 e_to = chunk * per + p
                 to = e_to * n_dp + d
-                block = y[pl.ds(d * rows, rows), p * cols:(p + 1) * cols]
+                block = y[pl.ds(d * rows, rows), starts[p]:starts[p] + span]
                 sendbuf[to] = fold(block).astype(jnp.bfloat16)
 
                 @pl.when(to != me)
@@ -157,13 +194,18 @@
         one = jnp.sum(jnp.where(ids == e, gates, 0.0), axis=1, keepdims=True)
         shares.append(jnp.concatenate([one, one], axis=0))
     pltpu.make_async_copy(recvbuf, recvbuf, out_recv).wait()
-    total = jnp.zeros((2 * rows, cols // 2), jnp.float32)
+    total = jnp.zeros((2 * rows, span // 2), jnp.float32)
     for e in range(n_exp):
-        part = jnp.zeros((2 * rows, cols // 2), jnp.float32)
+        part = jnp.zeros((2 * rows, span // 2), jnp.float32)
         for d in range(n_dp):
             part = part + recvbuf[e * n_dp + d].astype(jnp.float32)
         total = total + part * shares[e]
-    out_ref[...] = unfold(total).astype(out_ref.dtype)
+    wide = unfold(total)
+    for p in range(per):
+        @pl.when(e_me % per == p)
+        def _():
+            at = p * cols - starts[p]
+            out_ref[...] = wide[:, at:at + cols].astype(out_ref.dtype)
 
     pltpu.make_async_copy(
         tokbuf.at[pl.ds(0, n_all - 1)], tokbuf.at[pl.ds(0, n_all - 1)], tok_send
@@ -183,6 +225,7 @@
     while col_block % 128:
         col_block *= 2
     n_hid, n_col = hidden // hid_block, width // col_block
+    span = spans(cols, col_block)[1]
     vmem = pl.BlockSpec(memory_space=pltpu.VMEM)
     hbm = pl.BlockSpec(memory_space=pl.ANY)
     bf16, f32 = jnp.bfloat16, jnp.float32
@@ -200,8 +243,8 @@
             pltpu.VMEM((all_rows, width), bf16),
             pltpu.VMEM((n_hid, all_rows, hid_block), bf16),
             pltpu.VMEM((all_rows, col_block), f32),
-            pltpu.VMEM((n_all, 2 * rows, cols // 2), bf16),
-            pltpu.VMEM((n_all, 2 * rows, cols // 2), bf16),
+            pltpu.VMEM((n_all, 2 * rows, span // 2), bf16),
+            pltpu.VMEM((n_all, 2 * rows, span // 2), bf16),
             pltpu.SemaphoreType.DMA((n_hid,)),
             pltpu.SemaphoreType.DMA((n_hid,)),
             pltpu.SemaphoreType.DMA((n_col,)),

time: 43.2 us -> 35 us (0.81)
  Pallas kernels: 41.6 us -> 33.4 us
    pallas_call x1, Pallas kernels: 41.6 us -> 33.4 us  [local(): pl.pallas_call(functools.partial(kernel, n_exp, n_dp, hid_block, col_bloc...]
where the time goes in v2:
time: 35 us; the launch traced here: 34.7 us
  Pallas kernels  33.4 us (95%)
  local copies, waits for them, and re-layouts  1.3 us (4%)
    pallas_call x1, Pallas kernels, local(): pl.pallas_call(functools.partial(kernel, n_exp, n_dp, hid_block, col_bloc...  33.4 us
    unnamed x1, local copies, waits for them, and re-layouts  1.3 us

profile of v2, /device:TPU:0, one launch (start us, length us, event | category | flops | bytes accessed | tf_op | source)
XLA Modules:
  0.0 34.7 jit_solution(10092256512556688025)
XLA Ops:
  0.0 33.4 %shard_map.64 = bf16[8,448]{1,0:T(8,128)(2,1)} custom-call(bf16[8,448]{1,0:T(8,128)(2,1)} %tok_ref.1, s32[8,8]{1,0:T(8,128)} %ids_ref.1, f32[8,8]{1,0:T(8,128)} %gates_ref.1, bf16[1024,7168]{1,0:T(8,128)(2,1)} %bitcast.3, bf16[1024,7168]{1,0:T(8,128)(2,1)} %bitcast.4, bf16[1024,7168]{1,0:T(8,128)(2,1)} %bitcast.5), custom_call_target="tpu_custom_call" | custom-call | tf_op jit(solution)/shard_map/pallas_call | solution.py:232
  33.4 1.3 %copy.8 = bf16[8,448]{1,0:T(8,128)(2,1)} copy(bf16[8,448]{1,0:T(8,128)(2,1)} %shard_map.64) | data formatting | bytes 14336

commit v3 on v2

--- a/solution.py
+++ b/solution.py
@@ -49,7 +49,7 @@
     n_exp, n_dp, hid_block, col_block,
     tok_ref, ids_ref, gates_ref, wg_hbm, wu_hbm, wd_hbm, out_ref,
     wg, wu, wd, stage, tokbuf, x, hid, y, sendbuf, recvbuf,
-    g_sem, u_sem, d_sem, tok_send, tok_recv, out_send, out_recv,
+    g_sem, u_sem, d_sem, fwd_send, fwd_recv, tok_send, tok_recv, out_send, out_recv,
 ):
     n_all = n_exp * n_dp
     rows, cols = tok_ref.shape
@@ -115,29 +115,43 @@
         start_step(i)
 
     stage[...] = fold(tok_ref[...].astype(jnp.float32)).astype(jnp.bfloat16)
-    own = pltpu.make_async_copy(stage, tokbuf.at[me], tok_recv)
+    side = e_me % 2
+    n_side = n_all // 2
+    slot = e_me // 2 * n_dp + d_me
+    own = pltpu.make_async_copy(stage, tokbuf.at[side, slot], tok_recv)
     own.start()
     pl.semaphore_wait(barrier, n_all - 1)
 
-    @pl.loop(1, n_all)
+    @pl.loop(1, n_side)
     def _(k):
-        to = (me + k) % n_all
+        to = (slot + k) % n_side
         pltpu.make_async_remote_copy(
-            src_ref=stage, dst_ref=tokbuf.at[me], send_sem=tok_send, recv_sem=tok_recv,
-            device_id=(to // n_dp, to % n_dp), device_id_type=MESH,
+            src_ref=stage, dst_ref=tokbuf.at[side, slot], send_sem=tok_send,
+            recv_sem=tok_recv, device_id=(to // n_dp * 2 + side, to % n_dp),
+            device_id_type=MESH,
         ).start()
 
-    for i in range(early):
+    def early_step(i):
         copy_gate(i).wait()
         copy_up(i).wait()
         start_step(i + AHEAD)
-    pltpu.make_async_copy(tokbuf, tokbuf, tok_recv).wait()
+
+    early_step(0)
+    pltpu.make_async_copy(tokbuf.at[side], tokbuf.at[side], tok_recv).wait()
+    forward = pltpu.make_async_remote_copy(
+        src_ref=tokbuf.at[side], dst_ref=tokbuf.at[side], send_sem=fwd_send,
+        recv_sem=fwd_recv, device_id=(e_me + 1 - 2 * side, d_me), device_id_type=MESH,
+    )
+    forward.start()
+    for i in range(1, early):
+        early_step(i)
+    pltpu.make_async_copy(tokbuf.at[side], tokbuf.at[side], fwd_recv).wait()
 
     def gather_rows(pair):
         halves = []
         for q in range(2):
             parts = [
-                unfold(tokbuf[e * n_dp + pair * 2 + q].astype(jnp.float32))
+                unfold(tokbuf[e % 2, e // 2 * n_dp + pair * 2 + q].astype(jnp.float32))
                 for e in range(n_exp)
             ]
             halves.append(jnp.concatenate(parts, axis=1))
@@ -146,9 +160,8 @@
 
     each(n_dp // 2, gather_rows)
 
-    @pl.loop(0, n_hid)
-    def _(i):
-        @pl.when(i >= early)
+    def hid_step(i):
+        @pl.when(jnp.int32(i) >= early)
         def _():
             copy_gate(i).wait()
             copy_up(i).wait()
@@ -157,6 +170,8 @@
         gate = against_features(x[...], wg[i])
         upper = against_features(x[...], wu[i])
         hid[i] = (gate / (1.0 + jnp.exp(-gate)) * upper).astype(jnp.bfloat16)
+
+    each(n_hid, hid_step)
 
     @pl.loop(0, n_col)
     def _(i):
@@ -208,8 +223,9 @@
             out_ref[...] = wide[:, at:at + cols].astype(out_ref.dtype)
 
     pltpu.make_async_copy(
-        tokbuf.at[pl.ds(0, n_all - 1)], tokbuf.at[pl.ds(0, n_all - 1)], tok_send
+        tokbuf.at[0, pl.ds(0, n_side - 1)], tokbuf.at[0, pl.ds(0, n_side - 1)], tok_send
     ).wait()
+    pltpu.make_async_copy(tokbuf.at[side], tokbuf.at[side], fwd_send).wait()
     pltpu.make_async_copy(
         sendbuf.at[pl.ds(0, n_all - 1)], sendbuf.at[pl.ds(0, n_all - 1)], out_send
     ).wait()
@@ -239,7 +255,7 @@
             pltpu.VMEM((n_hid, hid_block, width), bf16),
             pltpu.VMEM((n_col, hidden, col_block), bf16),
             pltpu.VMEM((2 * rows, cols // 2), bf16),
-            pltpu.VMEM((n_all, 2 * rows, cols // 2), bf16),
+            pltpu.VMEM((2, n_all // 2, 2 * rows, cols // 2), bf16),
             pltpu.VMEM((all_rows, width), bf16),
             pltpu.VMEM((n_hid, all_rows, hid_block), bf16),
             pltpu.VMEM((all_rows, col_block), f32),
@@ -252,6 +268,8 @@
             pltpu.SemaphoreType.DMA,
             pltpu.SemaphoreType.DMA,
             pltpu.SemaphoreType.DMA,
+            pltpu.SemaphoreType.DMA,
+            pltpu.SemaphoreType.DMA,
         ],
         compiler_params=pltpu.CompilerParams(
             collective_id=0, has_side_effects=True, vmem_limit_bytes=56 * 1024 * 1024

time: 35 us -> 32.9 us (0.940)
  Pallas kernels: 33.4 us -> 31.4 us
    pallas_call x1, Pallas kernels: 33.4 us -> 31.4 us  [local(): pl.pallas_call(functools.partial(kernel, n_exp, n_dp, hid_block, col_bloc...]
where the time goes in v3:
time: 32.9 us; the launch traced here: 32.7 us
  Pallas kernels  31.4 us (95%)
  local copies, waits for them, and re-layouts  1.3 us (4%)
    pallas_call x1, Pallas kernels, local(): pl.pallas_call(functools.partial(kernel, n_exp, n_dp, hid_block, col_bloc...  31.4 us
    unnamed x1, local copies, waits for them, and re-layouts  1.3 us

profile of v3, /device:TPU:0, one launch (start us, length us, event | category | flops | bytes accessed | tf_op | source)
XLA Modules:
  0.0 32.7 jit_solution(10618446446547647335)
XLA Ops:
  0.0 31.4 %shard_map.64 = bf16[8,448]{1,0:T(8,128)(2,1)} custom-call(bf16[8,448]{1,0:T(8,128)(2,1)} %tok_ref.1, s32[8,8]{1,0:T(8,128)} %ids_ref.1, f32[8,8]{1,0:T(8,128)} %gates_ref.1, bf16[1024,7168]{1,0:T(8,128)(2,1)} %bitcast.3, bf16[1024,7168]{1,0:T(8,128)(2,1)} %bitcast.4, bf16[1024,7168]{1,0:T(8,128)(2,1)} %bitcast.5), custom_call_target="tpu_custom_call" | custom-call | tf_op jit(solution)/shard_map/pallas_call | solution.py:248
  31.4 1.3 %copy.8 = bf16[8,448]{1,0:T(8,128)(2,1)} copy(bf16[8,448]{1,0:T(8,128)(2,1)} %shard_map.64) | data formatting | bytes 14336
